TPU v7x, 512 devices: a whole 4x8x8 slice. The times are simulated.
512 devices in a mesh: ctx: 64 (over y, z), head: 8 (over x, core).
Axes of the slice: x: 4, y: 8, z: 8, core: 2. Of those that a mesh axis runs over, the one named last changes fastest.
Arguments:
- qkv_raw: bfloat16 [8192, 3, 2048], P('ctx', None, 'head'), may hold values from -6 to 6
- positions: int32 [8192], P('ctx'), may hold values from 0 to 8191, as said below
- filter_taps: float32 [3, 3, 2048], P(None, None, 'head'), may hold values from -1.2 to 1.2
- grad_out: bfloat16 [8192, 2048], P(('ctx', 'head')), may hold values from -6 to 6
Outputs:
- attn_out: bfloat16 [8192, 2048], P('ctx', 'head')
- qkv_grad: bfloat16 [8192, 3, 2048], P('ctx', None, 'head')
Inputs may be any that keep to these rules, and one draw needn't show every extreme that they name: Rows 128 d to 128 d + 127 hold, in increasing order, the positions of group c and then those of group 2 * 64 - 1 - c, each group being 64 consecutive positions, where c = (d + r) mod 64 with one r for the whole array; every position appears once.
All inputs are finite; a program needn't handle non-finite values.
Results may differ from a plain program's by a relative error of at most 0.03.
Values may be sent and summed in bfloat16 or wider, within the bound.
A program may use at most 64 MiB of HBM per device.

v0:
```python
import math
import jax
import jax.numpy as jnp
from jax import lax
from jax.sharding import PartitionSpec as P

HEAD_SIZE = 128
NEG_LARGE = -1e30


def extended_2(cells, sides, width):
    for axis, dim in sides:
        count = lax.axis_size(axis)
        head = lax.slice_in_dim(cells, 0, width, axis=dim)
        tail = lax.slice_in_dim(cells, cells.shape[dim] - width, cells.shape[dim], axis=dim)
        cells = jnp.concatenate(
            [
                lax.ppermute(tail, axis, [(i, (i + 1) % count) for i in range(count)]),
                cells,
                lax.ppermute(head, axis, [((i + 1) % count, i) for i in range(count)]),
            ],
            axis=dim,
        )
    return cells


def featurize(group_rows, prior_rows, filter_taps):
    rim_width = prior_rows.shape[0]
    row_count = group_rows.shape[0]
    extended = jnp.concatenate([prior_rows, group_rows], axis=0).astype(jnp.float32)
    result = jnp.zeros(group_rows.shape, jnp.float32)
    for tap_index in range(filter_taps.shape[1]):
        begin = rim_width - tap_index
        result = result + filter_taps[None, :, tap_index, :] * extended[begin : begin + row_count]
    return result


def unfeaturize(grad_rows, next_rows, filter_taps):
    row_count = grad_rows.shape[0]
    extended = jnp.concatenate([grad_rows, next_rows], axis=0)
    result = jnp.zeros(grad_rows.shape, jnp.float32)
    for tap_index in range(filter_taps.shape[1]):
        result = (
            result
            + filter_taps[None, :, tap_index, :] * extended[tap_index : tap_index + row_count]
        )
    return result


def locate_rows(first_row, row_count, group_len, pair_here, device_here, pair_count):
    row_ids = first_row + jnp.arange(row_count, dtype=jnp.int32)
    device_ids = row_ids // group_len
    pair_ids = (device_ids + pair_here - device_here) % pair_count
    offsets = row_ids % group_len
    early_pos = pair_ids * group_len + offsets
    late_pos = (2 * pair_count - 1 - pair_ids) * group_len + offsets
    return (early_pos, late_pos)


def split_product(left_wide, key_rows):
    high_part = left_wide.astype(jnp.bfloat16)
    rest_one = left_wide - high_part.astype(jnp.float32)
    middle_part = rest_one.astype(jnp.bfloat16)
    low_part = (rest_one - middle_part.astype(jnp.float32)).astype(jnp.bfloat16)
    total = jnp.einsum("hqk,khd->qhd", high_part, key_rows, preferred_element_type=jnp.float32)
    total = total + jnp.einsum(
        "hqk,khd->qhd", middle_part, key_rows, preferred_element_type=jnp.float32
    )
    return total + jnp.einsum(
        "hqk,khd->qhd", low_part, key_rows, preferred_element_type=jnp.float32
    )


def fresh_forward(row_count, head_count, head_size):
    return (
        jnp.full((head_count, row_count), NEG_LARGE, jnp.float32),
        jnp.zeros((head_count, row_count), jnp.float32),
        jnp.zeros((row_count, head_count, head_size), jnp.float32),
        jnp.zeros((row_count, head_count, head_size), jnp.float32),
        jnp.zeros((row_count, head_count, head_size), jnp.float32),
    )


def forward_update(
    carry_state, queries, query_pos, out_grads, key_rows, value_rows, key_pos, scaling
):
    running_max, running_sum, out_sum, weighted, plain_sum = carry_state
    scores = (
        jnp.einsum("qhd,khd->hqk", queries, key_rows, preferred_element_type=jnp.float32) * scaling
    )
    allowed = (key_pos[None, :] <= query_pos[:, None])[None]
    masked = jnp.where(allowed, scores, NEG_LARGE)
    new_max = jnp.maximum(running_max, jnp.max(masked, axis=2))
    factor = jnp.exp(running_max - new_max)
    weights = jnp.where(allowed, jnp.exp(masked - new_max[:, :, None]), 0.0)
    running_sum = running_sum * factor + jnp.sum(weights, axis=2)
    rescale = jnp.transpose(factor)[:, :, None]
    out_sum = out_sum * rescale + jnp.einsum(
        "hqk,khd->qhd", weights.astype(jnp.bfloat16), value_rows, preferred_element_type=jnp.float32
    )
    slopes = jnp.einsum("qhd,khd->hqk", out_grads, value_rows, preferred_element_type=jnp.float32)
    weighted = weighted * rescale + split_product(weights * slopes, key_rows)
    plain_sum = plain_sum * rescale + split_product(weights, key_rows)
    return (new_max, running_sum, out_sum, weighted, plain_sum)


def forward_finish(carry_state, out_grads, scaling):
    running_max, running_sum, out_sum, weighted, plain_sum = carry_state
    inverse = jnp.transpose(1.0 / running_sum)[:, :, None]
    attn = (out_sum * inverse).astype(jnp.bfloat16)
    log_total = jnp.transpose(running_max + jnp.log(running_sum))
    delta = jnp.sum(out_grads.astype(jnp.float32) * attn.astype(jnp.float32), axis=2)
    query_grad = scaling * (weighted - delta[:, :, None] * plain_sum) * inverse
    return (attn, log_total, delta, query_grad)


def forward_absorber(queries, out_grads, query_pos, locate, scaling):
    group_len = queries.shape[0] // 2
    head_count = queries.shape[1]
    head_size = queries.shape[2]

    def absorb(carried, block_in, first_row):
        key_block, value_block = block_in
        row_count = key_block.shape[1]
        step_rows = math.gcd(row_count, 256)

        def inner(step_index, state_pair):
            begin = step_index * step_rows
            key_part = lax.dynamic_slice_in_dim(key_block, begin, step_rows, 1).reshape(
                2, step_rows, head_count, head_size
            )
            value_part = lax.dynamic_slice_in_dim(value_block, begin, step_rows, 1).reshape(
                2, step_rows, head_count, head_size
            )
            early_pos, late_pos = locate(begin, step_rows)
            early_state, late_state = state_pair
            keys_both = key_part.reshape(2 * step_rows, head_count, head_size)
            values_both = value_part.reshape(2 * step_rows, head_count, head_size)
            pos_both = jnp.concatenate([early_pos, late_pos])
            late_state = forward_update(
                late_state,
                queries[group_len:],
                query_pos[group_len:],
                out_grads[group_len:],
                keys_both,
                values_both,
                pos_both,
                scaling,
            )
            early_state = forward_update(
                early_state,
                queries[:group_len],
                query_pos[:group_len],
                out_grads[:group_len],
                keys_both,
                values_both,
                pos_both,
                scaling,
            )
            return (early_state, late_state)

        return lax.fori_loop(0, row_count // step_rows, inner, carried)

    return absorb


def backward_update(
    grads_pair,
    key_rows,
    value_rows,
    key_pos,
    queries,
    out_grads,
    log_rows,
    delta_rows,
    query_pos,
    scaling,
):
    key_grad, value_grad = grads_pair
    scores = (
        jnp.einsum("qhd,khd->hqk", queries, key_rows, preferred_element_type=jnp.float32) * scaling
    )
    allowed = (key_pos[None, :] <= query_pos[:, None])[None]
    shifted = jnp.where(allowed, scores - jnp.transpose(log_rows)[:, :, None], NEG_LARGE)
    probs = jnp.where(allowed, jnp.exp(shifted), 0.0)
    value_grad = value_grad + jnp.einsum(
        "hqk,qhd->khd", probs.astype(jnp.bfloat16), out_grads, preferred_element_type=jnp.float32
    )
    slopes = jnp.einsum("qhd,khd->hqk", out_grads, value_rows, preferred_element_type=jnp.float32)
    dscores = (probs * (slopes - jnp.transpose(delta_rows)[:, :, None])).astype(jnp.bfloat16)
    key_grad = key_grad + jnp.einsum(
        "hqk,qhd->khd", dscores, queries, preferred_element_type=jnp.float32
    )
    return (key_grad, value_grad)


def backward_absorber(key_rows, value_rows, key_pos, locate, scaling):
    group_len = key_rows.shape[0] // 2
    head_count = key_rows.shape[1]
    head_size = key_rows.shape[2]

    def absorb(carried, block_in, first_row):
        query_block, grad_block, log_block, delta_block = block_in
        row_count = query_block.shape[1]
        step_rows = math.gcd(row_count, 256)

        def inner(step_index, grads_now):
            begin = step_index * step_rows
            query_part = lax.dynamic_slice_in_dim(query_block, begin, step_rows, 1).reshape(
                2, step_rows, head_count, head_size
            )
            grad_part = lax.dynamic_slice_in_dim(grad_block, begin, step_rows, 1).reshape(
                2, step_rows, head_count, head_size
            )
            log_part = lax.dynamic_slice_in_dim(log_block, begin, step_rows, 1)
            delta_part = lax.dynamic_slice_in_dim(delta_block, begin, step_rows, 1)
            early_pos, late_pos = locate(begin, step_rows)
            early_grads, late_grads = grads_now
            query_both = query_part.reshape(2 * step_rows, head_count, head_size)
            grad_both = grad_part.reshape(2 * step_rows, head_count, head_size)
            log_both = log_part.reshape(2 * step_rows, head_count)
            delta_both = delta_part.reshape(2 * step_rows, head_count)
            pos_both = jnp.concatenate([early_pos, late_pos])
            early_grads = backward_update(
                early_grads,
                key_rows[:group_len],
                value_rows[:group_len],
                key_pos[:group_len],
                query_both,
                grad_both,
                log_both,
                delta_both,
                pos_both,
                scaling,
            )
            late_grads = backward_update(
                late_grads,
                key_rows[group_len:],
                value_rows[group_len:],
                key_pos[group_len:],
                query_both,
                grad_both,
                log_both,
                delta_both,
                pos_both,
                scaling,
            )
            return (early_grads, late_grads)

        return lax.fori_loop(0, row_count // step_rows, inner, carried)

    return absorb


def local(qkv_raw, positions, filter_taps, grad_out):
    row_total = positions.shape[0]
    group_len = row_total // 2
    rim_width = filter_taps.shape[1] - 1
    channels = qkv_raw.shape[2]
    head_size = HEAD_SIZE
    head_count = channels // head_size
    scaling = 1.0 / math.sqrt(head_size)
    pair_count = lax.axis_size("ctx")
    device_here = lax.axis_index("ctx")
    pair_here = positions[0] // group_len

    def locate(first_row, row_count):
        return locate_rows(first_row, row_count, group_len, pair_here, device_here, pair_count)

    out_grads = lax.all_to_all(grad_out, "head", split_axis=1, concat_axis=0, tiled=True)
    early_rows = qkv_raw[:group_len]
    late_rows = qkv_raw[group_len:]
    early_tail = early_rows[group_len - rim_width :]
    late_tail = late_rows[group_len - rim_width :]
    tails = extended_2(jnp.concatenate([late_tail, early_tail], axis=0), (("ctx", 0),), rim_width)
    from_left = tails[:rim_width]
    from_right = tails[tails.shape[0] - rim_width :]
    early_prior = jnp.where(pair_here == 0, jnp.zeros_like(from_left), from_left)
    late_prior = jnp.where(pair_here == pair_count - 1, early_tail, from_right)
    featured = jnp.concatenate(
        [
            featurize(early_rows, early_prior, filter_taps),
            featurize(late_rows, late_prior, filter_taps),
        ],
        axis=0,
    ).astype(jnp.bfloat16)
    query_rows = featured[:, 0]
    key_rows = featured[:, 1]
    value_rows = featured[:, 2]
    col_first = 0 * head_size
    col_last = col_first + head_count * head_size
    width_now = col_last - col_first
    query_heads = query_rows.reshape(row_total, head_count, head_size)
    grad_heads = out_grads.reshape(row_total, head_count, head_size)
    initial = (
        fresh_forward(group_len, head_count, head_size),
        fresh_forward(group_len, head_count, head_size),
    )
    absorb = forward_absorber(query_heads, grad_heads, positions, locate, scaling)
    early_state, late_state = absorb(
        initial,
        (
            lax.all_gather(key_rows.reshape(2, group_len, width_now), "ctx", axis=1, tiled=True),
            lax.all_gather(value_rows.reshape(2, group_len, width_now), "ctx", axis=1, tiled=True),
        ),
        jnp.int32(0),
    )
    early_out = forward_finish(early_state, grad_heads[:group_len], scaling)
    late_out = forward_finish(late_state, grad_heads[group_len:], scaling)
    attn = jnp.concatenate([early_out[0], late_out[0]], axis=0)
    log_total = jnp.concatenate([early_out[1], late_out[1]], axis=0)
    delta = jnp.concatenate([early_out[2], late_out[2]], axis=0)
    query_grad = jnp.concatenate([early_out[3], late_out[3]], axis=0)
    absorb_back = backward_absorber(
        key_rows.reshape(row_total, head_count, head_size),
        value_rows.reshape(row_total, head_count, head_size),
        positions,
        locate,
        scaling,
    )
    zero_grads = (
        jnp.zeros((group_len, head_count, head_size), jnp.float32),
        jnp.zeros((group_len, head_count, head_size), jnp.float32),
    )
    early_grads, late_grads = absorb_back(
        (zero_grads, zero_grads),
        (
            lax.all_gather(
                query_rows.reshape(2, group_len, width_now).astype(jnp.float32),
                "ctx",
                axis=1,
                tiled=True,
            ).astype(jnp.bfloat16),
            lax.all_gather(
                out_grads.reshape(2, group_len, width_now).astype(jnp.float32),
                "ctx",
                axis=1,
                tiled=True,
            ).astype(jnp.bfloat16),
            lax.all_gather(log_total.reshape(2, group_len, head_count), "ctx", axis=1, tiled=True),
            lax.all_gather(delta.reshape(2, group_len, head_count), "ctx", axis=1, tiled=True),
        ),
        jnp.int32(0),
    )
    key_grad = scaling * jnp.concatenate([early_grads[0], late_grads[0]], axis=0)
    value_grad = jnp.concatenate([early_grads[1], late_grads[1]], axis=0)
    results = [(attn, query_grad, key_grad, value_grad)]
    attn_all = jnp.concatenate([entry[0] for entry in results], axis=1).reshape(row_total, channels)
    query_grad_all = jnp.concatenate([entry[1] for entry in results], axis=1).reshape(
        row_total, channels
    )
    key_grad_all = jnp.concatenate([entry[2] for entry in results], axis=1).reshape(
        row_total, channels
    )
    value_grad_all = jnp.concatenate([entry[3] for entry in results], axis=1).reshape(
        row_total, channels
    )
    post_grads = jnp.stack([query_grad_all, key_grad_all, value_grad_all], axis=1)
    early_head = post_grads[:rim_width]
    late_head = post_grads[group_len : group_len + rim_width]
    heads_rim = extended_2(
        jnp.concatenate([early_head, late_head], axis=0), (("ctx", 0),), rim_width
    )
    grad_left = heads_rim[:rim_width]
    grad_right = heads_rim[heads_rim.shape[0] - rim_width :]
    early_next = jnp.where(pair_here == pair_count - 1, late_head, grad_right)
    late_next = jnp.where(pair_here == 0, jnp.zeros_like(grad_left), grad_left)
    raw_grads = jnp.concatenate(
        [
            unfeaturize(post_grads[:group_len], early_next, filter_taps),
            unfeaturize(post_grads[group_len:], late_next, filter_taps),
        ],
        axis=0,
    )
    return (attn_all, raw_grads.astype(jnp.bfloat16))


def solution(mesh):
    in_specs = (P("ctx", None, "head"), P("ctx"), P(None, None, "head"), P(("ctx", "head"), None))
    out_specs = (P("ctx", "head"), P("ctx", None, "head"))
    return jax.shard_map(local, mesh=mesh, in_specs=in_specs, out_specs=out_specs, check_vma=False)
```

profile of v0, /device:TPU:4, one launch (start us, length us, event | category | flops | bytes accessed | tf_op | source)
XLA Modules:
  0.0 526.5 jit_solution(4368539386016358668)
XLA Ops:
  7.9 13.8 %collective-permute-start.1 = (bf16[2,3,256]{2,0,1:T(2,128)(2,1)S(1)}, bf16[2,3,256]{2,0,1:T(2,128)(2,1)S(1)}, u32[]{:S(2)}, u32[]{:S(2)}) collective-permute-start(bf16[2,3,256]{2,0,1:T(2,128)(2,1)S(1)} %slice.223), channel_id=1, source_target_pairs={{8,0},{16,8},{24,16},{32,24},{40,32},{48,40},{56,48},{64,56},{72,6... | collective-permute-start | bytes 9224 | tf_op jit(solution)/shard_map/ppermute | solution.py:20
  26.9 1.9 collective-permute-start
  28.9 6.8 %collective-permute-done = bf16[2,3,256]{2,0,1:T(2,128)(2,1)S(1)} collective-permute-done((bf16[2,3,256]{2,0,1:T(2,128)(2,1)S(1)}, bf16[2,3,256]{2,0,1:T(2,128)(2,1)S(1)}, u32[]{:S(2)}, u32[]{:S(2)}) %collective-permute-start) | collective-permute-done | bytes 3104 | tf_op jit(solution)/shard_map/ppermute | solution.py:18
  38.1 1.5 copy.311
  39.6 4.8 all-to-all-start
  48.1 68.9 %all-gather.5.cloned.1.call-done = bf16[2,4096,256]{2,1,0:T(8,128)(2,1)} async-done(((bf16[2,64,256]{2,1,0:T(8,128)(2,1)}), bf16[2,4096,256]{2,1,0:T(8,128)(2,1)}) %all-gather.5.cloned.1.call-update) | async-done | bytes 4194320 | tf_op jit(solution)/shard_map/all_gather | solution.py:303
  117.0 87.5 %all-gather.7.cloned.1.call-done = bf16[2,4096,256]{2,1,0:T(8,128)(2,1)} async-done(((bf16[2,64,256]{2,1,0:T(8,128)(2,1)}), bf16[2,4096,256]{2,1,0:T(8,128)(2,1)}) %all-gather.7.cloned.1.call-update) | async-done | bytes 4194320 | tf_op jit(solution)/shard_map/all_gather | solution.py:304
  204.5 114.2 %while.56 = (s32[]{:T(128)}, f32[2,64]{1,0:T(2,128)S(1)}, f32[2,64]{1,0:T(2,128)S(1)}, f32[64,2,128]{2,0,1:T(8,128)S(1)}, f32[64,2,128]{2,0,1:T(8,128)S(1)}, /*i...) while((s32[]{:T(128)}, f32[2,64]{1,0:T(2,128)S(1)}, ...), condition=%wide.region_5.6_spmd.clone, body=%wide.region_0.5_spmd.clone.sunk | while | flops 308006656 | bytes 15106853 | solution.py:162
  320.3 66.3 %all_gather.23 = f32[2,4096,2]{2,0,1:T(2,128)} all-gather(f32[2,64,2]{2,0,1:T(2,128)S(1)} %copy.224), channel_id=1, replica_groups=mesh['ctx'=64,'head'=8] {'ctx'}, dimensions={1}, use_global_device_ids=true | all-gather | bytes 66560 | tf_op jit(solution)/shard_map/all_gather | solution.py:341
  386.6 5.2 copy.228
  392.1 56.2 %all_gather.21 = f32[2,4096,2]{2,0,1:T(2,128)} all-gather(f32[2,64,2]{2,0,1:T(2,128)S(1)} %copy.221), channel_id=1, replica_groups=mesh['ctx'=64,'head'=8] {'ctx'}, dimensions={1}, use_global_device_ids=true | all-gather | bytes 66560 | tf_op jit(solution)/shard_map/all_gather | solution.py:340
  448.3 5.1 copy.226
  454.2 49.3 %while.57 = (s32[]{:T(128)}, f32[64,2,128]{2,0,1:T(8,128)S(1)}, f32[64,2,128]{2,0,1:T(8,128)S(1)}, f32[64,2,128]{2,0,1:T(8,128)S(1)}, f32[64,2,128]{2,0,1:T(8,12...) while((s32[]{:T(128)}, f32[64,2,128]{2,0,1:T(8,128)S(1)}, ...), condition=%wide.region_9.10_spmd.clone, body=%wide.region_8.9_spmd.clone.sunk | while | flops 135473152 | bytes 6612724 | solution.py:250
  457.3 1.1 constant_dynamic-slice_fusion.9
  460.4 1.1 constant_dynamic-slice_fusion.9
  463.5 1.1 constant_dynamic-slice_fusion.9
  466.6 1.1 constant_dynamic-slice_fusion.9
  469.7 1.1 constant_dynamic-slice_fusion.9
  472.7 1.1 constant_dynamic-slice_fusion.9
  475.8 1.1 constant_dynamic-slice_fusion.9
  478.9 1.1 constant_dynamic-slice_fusion.9
  482.0 1.1 constant_dynamic-slice_fusion.9
  485.1 1.1 constant_dynamic-slice_fusion.9
  488.2 1.1 constant_dynamic-slice_fusion.9
  491.3 1.1 constant_dynamic-slice_fusion.9
  494.3 1.1 constant_dynamic-slice_fusion.9
  497.4 1.1 constant_dynamic-slice_fusion.9
  500.5 1.1 constant_dynamic-slice_fusion.9
  504.1 4.6 collective-permute-start.2
  508.7 1.3 collective-permute-done.2
  510.0 2.1 collective-permute-start.3
  512.2 6.9 %collective-permute-done.3 = f32[2,3,256]{2,0,1:T(2,128)S(1)} collective-permute-done((f32[2,3,256]{2,0,1:T(2,128)S(1)}, f32[2,3,256]{2,0,1:T(2,128)S(1)}, u32[]{:S(2)}, u32[]{:S(2)}) %collective-permute-start.3) | collective-permute-done | bytes 6176 | tf_op jit(solution)/shard_map/ppermute | solution.py:18
  (875 shorter events, 155.7 us)
Async XLA Ops:
  7.2 197.4 %copy-start.1 = (s32[128]{0:T(128)S(1)}, s32[128]{0:T(128)}, u32[]{:S(2)}) copy-start(s32[128]{0:T(128)} %param.9) | copy-start | bytes 1540
  7.2 109.8 %all-gather.5.cloned.1.call-start = ((), (), s32[]{:S(2)}) async-start(), calls=%async_computation.1 | async-start | bytes 4259840 | tf_op jit(solution)/shard_map/all_gather | solution.py:303
  7.9 18.3 %collective-permute-start.1 = (bf16[2,3,256]{2,0,1:T(2,128)(2,1)S(1)}, bf16[2,3,256]{2,0,1:T(2,128)(2,1)S(1)}, u32[]{:S(2)}, u32[]{:S(2)}) collective-permute-start(bf16[2,3,256]{2,0,1:T(2,128)(2,1)S(1)} %slice.223), channel_id=1, source_target_pairs={{8,0},{16,8},{24,16},{32,24},{40,32},{48,40},{56,48},{64,56},{72,6... | collective-permute-start | bytes 9224 | tf_op jit(solution)/shard_map/ppermute | solution.py:20
  26.9 8.8 %collective-permute-start = (bf16[2,3,256]{2,0,1:T(2,128)(2,1)S(1)}, bf16[2,3,256]{2,0,1:T(2,128)(2,1)S(1)}, u32[]{:S(2)}, u32[]{:S(2)}) collective-permute-start(bf16[2,3,256]{2,0,1:T(2,128)(2,1)S(1)} %get-tuple-element.1180), channel_id=1, source_target_pairs={{0,8},{8,16},{16,24},{24,32},{32,40},{40,48},{48,56},{56,64},{64,7... | collective-permute-start | bytes 9224 | tf_op jit(solution)/shard_map/ppermute | solution.py:18
  36.6 167.9 %all-gather.7.cloned.1.call-start = ((), (), s32[]{:S(2)}) async-start(), calls=%async_computation.2 | async-start | bytes 4259840 | tf_op jit(solution)/shard_map/all_gather | solution.py:304
  37.4 416.8 %all-gather.9.cloned.1.call-start = ((), (), s32[]{:S(2)}) async-start(), calls=%async_computation.3 | async-start | bytes 4259840 | tf_op jit(solution)/shard_map/all_gather | solution.py:328
  39.6 7.9 %all-to-all-start = ((bf16[16,8,256]{2,0,1:T(8,128)(2,1)}), bf16[16,8,256]{2,0,1:T(8,128)(2,1)S(1)}, u32[]{:S(2)}, u32[]{:S(2)}) async-start(bf16[16,8,256]{2,0,1:T(8,128)(2,1)} %bitcast.116), calls=%async_computation | async-start | bytes 131072 | tf_op jit(solution)/shard_map/all_to_all | solution.py:270
  44.4 409.8 %all-gather.11.cloned.1.call-start = ((), (), s32[]{:S(2)}) async-start(), calls=%async_computation.4 | async-start | bytes 4259840 | tf_op jit(solution)/shard_map/all_gather | solution.py:334
  47.5 0.6 copy-start
  504.1 5.9 %collective-permute-start.2 = (f32[2,3,256]{2,0,1:T(2,128)S(1)}, f32[2,3,256]{2,0,1:T(2,128)S(1)}, u32[]{:S(2)}, u32[]{:S(2)}) collective-permute-start(f32[2,3,256]{2,0,1:T(2,128)S(1)} %pad_maximum_fusion.8), channel_id=1, source_target_pairs={{8,0},{16,8},{24,16},{32,24},{40,32},{48,40},{56,48},{64,56},{72,6... | collective-permute-start | bytes 18440 | tf_op jit(solution)/shard_map/ppermute | solution.py:20
  510.0 9.1 %collective-permute-start.3 = (f32[2,3,256]{2,0,1:T(2,128)S(1)}, f32[2,3,256]{2,0,1:T(2,128)S(1)}, u32[]{:S(2)}, u32[]{:S(2)}) collective-permute-start(f32[2,3,256]{2,0,1:T(2,128)S(1)} %get-tuple-element.1145), channel_id=1, source_target_pairs={{0,8},{8,16},{16,24},{24,32},{32,40},{40,48},{48,56},{56,64},{64,7... | collective-permute-start | bytes 18440 | tf_op jit(solution)/shard_map/ppermute | solution.py:18
Sparse Core Ops, SparseCore 0:
  36.8 80.2 all-gather.4
  120.7 83.8 all-gather.6
  207.6 84.1 all-gather.8
  294.7 92.4 all-gather.10
where the time goes:
time: 529 us; the launch traced here: 526 us
  waiting for transfers between devices  173 us (33%)
  blocking collectives  123 us (23%)
  matrix products  91.4 us (17%)
  local copies, waits for them, and re-layouts  75.1 us (14%)
  starting transfers between devices  27.4 us (5%)
  between operations  16.8 us (3%)
  other arithmetic  15.2 us (3%)
    all_gather x1, waiting for transfers between devices, local(): lax.all_gather(value_rows.reshape(2, group_len, width_now), 'ctx', axis=1...  87.5 us
    all_gather x1, waiting for transfers between devices, local(): lax.all_gather(key_rows.reshape(2, group_len, width_now), 'ctx', axis=1,...  68.9 us
    all_gather x1, blocking collectives, local(): lax.all_gather(delta.reshape(2, group_len, head_count), 'ctx', axis=1, ti...  66.3 us
    all_gather x1, blocking collectives, local(): lax.all_gather(log_total.reshape(2, group_len, head_count), 'ctx', axis=1...  56.2 us
    ppermute x2, starting transfers between devices, extended_2(): lax.ppermute(head, axis, [((i + 1) % count, i) for i in range(count)])  18.4 us
    dynamic_slice x16, local copies, waits for them, and re-layouts, inner(): lax.dynamic_slice_in_dim(grad_block, begin, step_rows, 1)  17.2 us
    dynamic_slice x16, local copies, waits for them, and re-layouts, inner(): lax.dynamic_slice_in_dim(value_block, begin, step_rows, 1)  15.7 us
    dynamic_slice x16, local copies, waits for them, and re-layouts, inner(): lax.dynamic_slice_in_dim(key_block, begin, step_rows, 1)  15.6 us
  transfers between devices with their start and end apart: 9, of which 6 were waited for; matrix products, arithmetic and copies ran while one was open for 25% of the time, Pallas kernels for 0%

commit v1 on v0

--- a/solution.py
+++ b/solution.py
@@ -6,6 +6,13 @@
 
 HEAD_SIZE = 128
 NEG_LARGE = -1e30
+
+
+def all_by_exchange(block, axis, dim):
+    devices = lax.axis_size(axis)
+    blocks = jnp.stack([block for _ in range(devices)])
+    blocks = lax.all_to_all(blocks, axis, split_axis=0, concat_axis=0)
+    return jnp.concatenate(blocks, axis=dim)
 
 
 def extended_2(cells, sides, width):
@@ -301,7 +308,7 @@
         initial,
         (
             lax.all_gather(key_rows.reshape(2, group_len, width_now), "ctx", axis=1, tiled=True),
-            lax.all_gather(value_rows.reshape(2, group_len, width_now), "ctx", axis=1, tiled=True),
+            all_by_exchange(value_rows.reshape(2, group_len, width_now), "ctx", 1),
         ),
         jnp.int32(0),
     )

time: 529 us -> 558 us (1.055)
  the two profiles are of different devices: /device:TPU:4 before, /device:TPU:6 now
where the time goes in v1:
time: 558 us; the launch traced here: 555 us
  waiting for transfers between devices  192 us (34%)
  blocking collectives  122 us (22%)
  matrix products  91.3 us (16%)
  local copies, waits for them, and re-layouts  79.3 us (14%)
  starting transfers between devices  33.2 us (6%)
  between operations  16.9 us (3%)
  other arithmetic  15.2 us (3%)
    all_to_all x1, waiting for transfers between devices, all_by_exchange(): blocks = lax.all_to_all(blocks, axis, split_axis=0, concat_axis=0)  111 us
    all_gather x1, blocking collectives, local(): lax.all_gather(delta.reshape(2, group_len, head_count), 'ctx', axis=1, ti...  66.4 us
    all_gather x1, waiting for transfers between devices, local(): lax.all_gather(key_rows.reshape(2, group_len, width_now), 'ctx', axis=1,...  62.3 us
    all_gather x1, blocking collectives, local(): lax.all_gather(log_total.reshape(2, group_len, head_count), 'ctx', axis=1...  56.1 us
    ppermute x2, starting transfers between devices, extended_2(): lax.ppermute(head, axis, [((i + 1) % count, i) for i in range(count)])  18.4 us
    dynamic_slice x16, local copies, waits for them, and re-layouts, inner(): lax.dynamic_slice_in_dim(grad_block, begin, step_rows, 1)  17.2 us
    dynamic_slice x16, local copies, waits for them, and re-layouts, inner(): lax.dynamic_slice_in_dim(value_block, begin, step_rows, 1)  15.7 us
    dynamic_slice x16, local copies, waits for them, and re-layouts, inner(): lax.dynamic_slice_in_dim(key_block, begin, step_rows, 1)  15.6 us
  transfers between devices with their start and end apart: 9, of which 6 were waited for; matrix products, arithmetic and copies ran while one was open for 24% of the time, Pallas kernels for 0%

profile of v1, /device:TPU:6, one launch (start us, length us, event | category | flops | bytes accessed | tf_op | source)
XLA Modules:
  0.0 555.2 jit_solution(3535764443972508873)
XLA Ops:
  7.9 13.8 %collective-permute-start.1 = (bf16[2,3,256]{2,0,1:T(2,128)(2,1)S(1)}, bf16[2,3,256]{2,0,1:T(2,128)(2,1)S(1)}, u32[]{:S(2)}, u32[]{:S(2)}) collective-permute-start(bf16[2,3,256]{2,0,1:T(2,128)(2,1)S(1)} %slice.223), channel_id=1, source_target_pairs={{8,0},{16,8},{24,16},{32,24},{40,32},{48,40},{56,48},{64,56},{72,6... | collective-permute-start | bytes 9224 | tf_op jit(solution)/shard_map/ppermute | solution.py:27
  26.9 1.9 collective-permute-start
  28.9 6.8 %collective-permute-done = bf16[2,3,256]{2,0,1:T(2,128)(2,1)S(1)} collective-permute-done((bf16[2,3,256]{2,0,1:T(2,128)(2,1)S(1)}, bf16[2,3,256]{2,0,1:T(2,128)(2,1)S(1)}, u32[]{:S(2)}, u32[]{:S(2)}) %collective-permute-start) | collective-permute-done | bytes 3104 | tf_op jit(solution)/shard_map/ppermute | solution.py:25
  36.6 1.5 copy.314
  38.1 4.8 all-to-all-start.1
  43.6 2.8 all-to-all-done.1
  46.4 2.5 stack.6
  48.9 5.8 %all-to-all-start = ((bf16[64,2,64,256]{3,2,1,0:T(8,128)(2,1)}), bf16[64,2,64,256]{3,2,1,0:T(8,128)(2,1)}, u32[]{:S(2)}, u32[]{:S(2)}) async-start(bf16[64,2,64,256]{3,2,1,0:T(8,128)(2,1)} %stack.6), calls=%async_computation | async-start | bytes 8388608 | tf_op jit(solution)/shard_map/all_to_all | solution.py:14
  55.5 111.0 %all-to-all-done = bf16[64,2,64,256]{3,2,1,0:T(8,128)(2,1)} async-done(((bf16[64,2,64,256]{3,2,1,0:T(8,128)(2,1)}), bf16[64,2,64,256]{3,2,1,0:T(8,128)(2,1)}, u32[]{:S(2)}, u32[]{:S(2)}) %all-to-all-start) | async-done | bytes 4194336 | tf_op jit(solution)/shard_map/all_to_all | solution.py:14
  166.5 4.7 copy.213
  171.2 62.3 %all-gather.4.cloned.1.call-done = bf16[2,4096,256]{2,1,0:T(8,128)(2,1)} async-done(((bf16[2,64,256]{2,1,0:T(8,128)(2,1)}), bf16[2,4096,256]{2,1,0:T(8,128)(2,1)}) %all-gather.4.cloned.1.call-update) | async-done | bytes 4194320 | tf_op jit(solution)/shard_map/all_gather | solution.py:310
  233.5 114.1 %while.56 = (s32[]{:T(128)}, f32[2,64]{1,0:T(2,128)S(1)}, f32[2,64]{1,0:T(2,128)S(1)}, f32[64,2,128]{2,0,1:T(8,128)S(1)}, f32[64,2,128]{2,0,1:T(8,128)S(1)}, /*i...) while((s32[]{:T(128)}, f32[2,64]{1,0:T(2,128)S(1)}, ...), condition=%wide.region_5.6_spmd.clone, body=%wide.region_0.5_spmd.clone.sunk | while | flops 308006656 | bytes 15106853 | solution.py:169
  349.2 66.4 %all_gather.19 = f32[2,4096,2]{2,0,1:T(2,128)} all-gather(f32[2,64,2]{2,0,1:T(2,128)S(1)} %copy.227), channel_id=1, replica_groups=mesh['ctx'=64,'head'=8] {'ctx'}, dimensions={1}, use_global_device_ids=true | all-gather | bytes 66560 | tf_op jit(solution)/shard_map/all_gather | solution.py:348
  415.6 5.2 copy.231
  421.0 56.1 %all_gather.17 = f32[2,4096,2]{2,0,1:T(2,128)} all-gather(f32[2,64,2]{2,0,1:T(2,128)S(1)} %copy.224), channel_id=1, replica_groups=mesh['ctx'=64,'head'=8] {'ctx'}, dimensions={1}, use_global_device_ids=true | all-gather | bytes 66560 | tf_op jit(solution)/shard_map/all_gather | solution.py:347
  477.1 5.1 copy.229
  483.0 49.3 %while.57 = (s32[]{:T(128)}, f32[64,2,128]{2,0,1:T(8,128)S(1)}, f32[64,2,128]{2,0,1:T(8,128)S(1)}, f32[64,2,128]{2,0,1:T(8,128)S(1)}, f32[64,2,128]{2,0,1:T(8,12...) while((s32[]{:T(128)}, f32[64,2,128]{2,0,1:T(8,128)S(1)}, ...), condition=%wide.region_9.10_spmd.clone, body=%wide.region_8.9_spmd.clone.sunk | while | flops 135473152 | bytes 6612724 | solution.py:257
  486.1 1.1 constant_dynamic-slice_fusion.9
  489.1 1.1 constant_dynamic-slice_fusion.9
  492.2 1.1 constant_dynamic-slice_fusion.9
  495.3 1.1 constant_dynamic-slice_fusion.9
  498.4 1.1 constant_dynamic-slice_fusion.9
  501.5 1.1 constant_dynamic-slice_fusion.9
  504.6 1.1 constant_dynamic-slice_fusion.9
  507.7 1.1 constant_dynamic-slice_fusion.9
  510.7 1.1 constant_dynamic-slice_fusion.9
  513.8 1.1 constant_dynamic-slice_fusion.9
  529.3 1.1 constant_dynamic-slice_fusion.9
  532.8 4.6 collective-permute-start.2
  537.5 1.3 collective-permute-done.2
  538.8 2.3 collective-permute-start.3
  541.1 6.8 %collective-permute-done.3 = f32[2,3,256]{2,0,1:T(2,128)S(1)} collective-permute-done((f32[2,3,256]{2,0,1:T(2,128)S(1)}, f32[2,3,256]{2,0,1:T(2,128)S(1)}, u32[]{:S(2)}, u32[]{:S(2)}) %collective-permute-start.3) | collective-permute-done | bytes 6176 | tf_op jit(solution)/shard_map/ppermute | solution.py:25
  (880 shorter events, 156.0 us)
Async XLA Ops:
  7.2 226.4 %all-gather.4.cloned.1.call-start = ((), (), s32[]{:S(2)}) async-start(), calls=%async_computation.2 | async-start | bytes 4259840 | tf_op jit(solution)/shard_map/all_gather | solution.py:310
  7.9 18.3 %collective-permute-start.1 = (bf16[2,3,256]{2,0,1:T(2,128)(2,1)S(1)}, bf16[2,3,256]{2,0,1:T(2,128)(2,1)S(1)}, u32[]{:S(2)}, u32[]{:S(2)}) collective-permute-start(bf16[2,3,256]{2,0,1:T(2,128)(2,1)S(1)} %slice.223), channel_id=1, source_target_pairs={{8,0},{16,8},{24,16},{32,24},{40,32},{48,40},{56,48},{64,56},{72,6... | collective-permute-start | bytes 9224 | tf_op jit(solution)/shard_map/ppermute | solution.py:27
  26.9 8.8 %collective-permute-start = (bf16[2,3,256]{2,0,1:T(2,128)(2,1)S(1)}, bf16[2,3,256]{2,0,1:T(2,128)(2,1)S(1)}, u32[]{:S(2)}, u32[]{:S(2)}) collective-permute-start(bf16[2,3,256]{2,0,1:T(2,128)(2,1)S(1)} %get-tuple-element.1180), channel_id=1, source_target_pairs={{0,8},{8,16},{16,24},{24,32},{32,40},{40,48},{48,56},{56,64},{64,7... | collective-permute-start | bytes 9224 | tf_op jit(solution)/shard_map/ppermute | solution.py:25
  38.1 8.3 %all-to-all-start.1 = ((bf16[16,8,256]{2,0,1:T(8,128)(2,1)}), bf16[16,8,256]{2,0,1:T(8,128)(2,1)S(1)}, u32[]{:S(2)}, u32[]{:S(2)}) async-start(bf16[16,8,256]{2,0,1:T(8,128)(2,1)} %bitcast.119), calls=%async_computation.1 | async-start | bytes 131072 | tf_op jit(solution)/shard_map/all_to_all | solution.py:277
  42.9 440.1 %all-gather.6.cloned.1.call-start = ((), (), s32[]{:S(2)}) async-start(), calls=%async_computation.3 | async-start | bytes 4259840 | tf_op jit(solution)/shard_map/all_gather | solution.py:335
  46.4 8.7 %copy-start = (bf16[16,8,256]{2,0,1:T(8,128)(2,1)}, bf16[16,8,256]{2,0,1:T(8,128)(2,1)S(1)}, u32[]{:S(2)}) copy-start(bf16[16,8,256]{2,0,1:T(8,128)(2,1)S(1)} %all-to-all-done.1) | copy-start | bytes 196612
  48.9 6.0 %copy-start.1 = (bf16[128,1,256]{2,0,1:T(8,128)(2,1)S(1)}, bf16[128,1,256]{2,0,1:T(8,128)(2,1)}, u32[]{:S(2)}) copy-start(bf16[128,1,256]{2,0,1:T(8,128)(2,1)} %get-tuple-element.1178) | copy-start | bytes 196612
  48.9 6.0 %copy-start.2 = (bf16[128,1,256]{2,0,1:T(8,128)(2,1)S(1)}, bf16[128,1,256]{2,0,1:T(8,128)(2,1)}, u32[]{:S(2)}) copy-start(bf16[128,1,256]{2,0,1:T(8,128)(2,1)} %get-tuple-element.1177) | copy-start | bytes 196612
  48.9 117.6 %all-to-all-start = ((bf16[64,2,64,256]{3,2,1,0:T(8,128)(2,1)}), bf16[64,2,64,256]{3,2,1,0:T(8,128)(2,1)}, u32[]{:S(2)}, u32[]{:S(2)}) async-start(bf16[64,2,64,256]{3,2,1,0:T(8,128)(2,1)} %stack.6), calls=%async_computation | async-start | bytes 8388608 | tf_op jit(solution)/shard_map/all_to_all | solution.py:14
  54.7 428.3 %all-gather.8.cloned.1.call-start = ((), (), s32[]{:S(2)}) async-start(), calls=%async_computation.4 | async-start | bytes 4259840 | tf_op jit(solution)/shard_map/all_gather | solution.py:341
  55.5 178.1 %copy-start.3 = (s32[128]{0:T(128)S(1)}, s32[128]{0:T(128)}, u32[]{:S(2)}) copy-start(s32[128]{0:T(128)} %param.9) | copy-start | bytes 1540
  532.8 5.9 %collective-permute-start.2 = (f32[2,3,256]{2,0,1:T(2,128)S(1)}, f32[2,3,256]{2,0,1:T(2,128)S(1)}, u32[]{:S(2)}, u32[]{:S(2)}) collective-permute-start(f32[2,3,256]{2,0,1:T(2,128)S(1)} %pad_maximum_fusion.8), channel_id=1, source_target_pairs={{8,0},{16,8},{24,16},{32,24},{40,32},{48,40},{56,48},{64,56},{72,6... | collective-permute-start | bytes 18440 | tf_op jit(solution)/shard_map/ppermute | solution.py:27
  538.8 9.1 %collective-permute-start.3 = (f32[2,3,256]{2,0,1:T(2,128)S(1)}, f32[2,3,256]{2,0,1:T(2,128)S(1)}, u32[]{:S(2)}, u32[]{:S(2)}) collective-permute-start(f32[2,3,256]{2,0,1:T(2,128)S(1)} %get-tuple-element.1145), channel_id=1, source_target_pairs={{0,8},{8,16},{16,24},{24,32},{32,40},{40,48},{48,56},{56,64},{64,7... | collective-permute-start | bytes 18440 | tf_op jit(solution)/shard_map/ppermute | solution.py:25
Sparse Core Ops, SparseCore 0:
  36.7 196.7 all-gather.3
  236.6 84.1 all-gather.5
  323.9 92.1 all-gather.7
